TPU v7x, 32 devices: a whole 2x2x4 slice. The times are simulated.
32 devices in a mesh: grp: 2 (over x), ka: 16 (over z, y, core).
Axes of the slice: x: 2, y: 2, z: 4, core: 2. Of those that a mesh axis runs over, the one named last changes fastest.
Arguments:
- left_amps: bfloat16 [32, 6656, 624], P(('grp', 'ka')), parts along dimension 0, may hold values from -6 to 6
- right_amps: bfloat16 [32, 3, 6656, 104], P('grp', None, 'ka'), parts along dimension 0, may hold values from -0.0390625 to 0.0390625
- allowed: int32 [32, 3], P('grp'), parts along dimension 0, may hold values 0 or 1
Outputs:
- density_vv: float32 [32, 64896], P(('grp', 'ka')), parts along dimension 0
- density_oo: float32 [32, 384], P(('grp', 'ka')), parts along dimension 0
There are 2 independent parts, one for each index of `grp`. A program takes and returns all parts, laid end to end along the dimension named above; each array names one. Nothing has to cross between parts.
All inputs are finite; a program needn't handle non-finite values.
Results may differ from a plain program's by a relative error of at most 0.0003.
Values may be sent and summed in bfloat16 or wider, within the bound.
A program may use at most 128 MiB of HBM per device.

v0:
```python
import jax
import jax.numpy as jnp
from jax import lax
from jax.sharding import PartitionSpec as P

NO = 8
NV = 104
NL = 6


def from_behind(shard, axis, by):
    length = lax.axis_size(axis)
    return lax.ppermute(shard, axis, [(i, (i + by) % length) for i in range(length)])


def contract(left_block, right_block):
    square = lax.dot_general(
        left_block, right_block, (((0,), (0,)), ((), ())), preferred_element_type=jnp.float32
    )
    left_view = left_block.reshape(NO, NO * NV, NL, NV)
    right_view = right_block.reshape(NO, NO * NV, NV)
    occupied = -jnp.einsum(
        "ipra,jpa->rij", left_view, right_view, preferred_element_type=jnp.float32
    )
    return (square.reshape(-1), occupied.reshape(-1))


def masked_term(left_block, right_block, permit):
    square, occupied = contract(left_block, right_block)
    factor = permit.astype(jnp.float32)
    return (square * factor, occupied * factor)


def local(left_amps, right_amps, allowed):
    window_count = right_amps.shape[1]
    middle = window_count // 2
    position = lax.axis_index("ka")
    relaid = lax.all_to_all(right_amps, "ka", split_axis=0, concat_axis=2, tiled=True)[0]
    left_block = left_amps[0]
    total_vv = jnp.zeros((NL * NV * NV,), jnp.float32)
    total_oo = jnp.zeros((NL * NO * NO,), jnp.float32)
    pieces = {0: left_block}
    forward = left_block
    distance = 1
    forward = from_behind(forward, "ka", -1)
    pieces[distance] = forward
    backward = left_block
    distance = 1
    backward = from_behind(backward, "ka", 1)
    pieces[-distance] = backward
    for window in range(window_count):
        offset = window - middle
        square, occupied = masked_term(pieces[offset], relaid[window], allowed[position, window])
        total_vv = total_vv + square
        total_oo = total_oo + occupied
    return (total_vv[None], total_oo[None])


def solution(mesh):
    in_specs = (P(("grp", "ka"), None, None), P("grp", None, "ka", None), P("grp", None))
    out_specs = (P(("grp", "ka"), None), P(("grp", "ka"), None))
    return jax.shard_map(local, mesh=mesh, in_specs=in_specs, out_specs=out_specs, check_vma=False)
```

profile of v0, /device:TPU:13, one launch (start us, length us, event | category | flops | bytes accessed | tf_op | source)
XLA Modules:
  0.0 343.0 jit_solution(10708991782346441775)
XLA Ops:
  0.6 6.6 %all-to-all-start = ((bf16[16,3,416,104]{3,2,1,0:T(8,128)(2,1)}), bf16[16,3,416,104]{3,2,1,0:T(8,128)(2,1)}, u32[]{:S(2)}, u32[]{:S(2)}) async-start(bf16[16,3,416,104]{3,2,1,0:T(8,128)(2,1)} %param.4), calls=%async_computation | async-start | bytes 10223616 | tf_op jit(solution)/shard_map/all_to_all | solution.py:38
  7.2 0.4 collective-permute-start.1
  7.6 2.3 collective-permute-start
  9.8 15.3 %reshape_squeeze.14 = bf16[8,832,6,104]{1,0,3,2:T(8,128)(2,1)} reshape(bf16[1,6656,624]{1,2,0:T(8,128)(2,1)} %param.3) | data formatting | bytes 16613376 | tf_op jit(solution)/shard_map/reshape;squeeze | solution.py:20
  25.1 0.6 constant_dynamic-slice_fusion.2
  27.7 181.1 %all-to-all-done = bf16[16,3,416,104]{3,2,1,0:T(8,128)(2,1)} async-done(((bf16[16,3,416,104]{3,2,1,0:T(8,128)(2,1)}), bf16[16,3,416,104]{3,2,1,0:T(8,128)(2,1)}, u32[]{:S(2)}, u32[]{:S(2)}) %all-to-all-start) | async-done | bytes 4153376 | tf_op jit(solution)/shard_map/all_to_all | solution.py:38
  208.8 4.0 %fusion.45 = (bf16[1,1,16,416,104]{4,3,1,2,0:T(8,128)(2,1)S(1)}, bf16[1,1,16,416,104]{4,3,1,2,0:T(8,128)(2,1)S(1)}, bf16[1,1,16,416,104]{4,3,1,2,0:T(8,128)(2,1)}) fusion(bf16[1,3,16,416,104]{4,3,1,2,0:T(8,128)(2,1)} %bitcast.2), kind=kLoop, calls=%fused_computation.27 | loop fusion | bytes 8306688 | tf_op jit(solution)/shard_map/slice | solution.py:53
  212.8 3.7 %copy.17 = bf16[8,832,104]{1,0,2:T(8,128)(2,1)} copy(bf16[8,832,104]{2,1,0:T(8,128)(2,1)} %bitcast.97) | data formatting | bytes 2768896 | tf_op jit(solution)/shard_map/reshape;squeeze | solution.py:21
  216.6 2.8 copy.18
  219.3 2.8 copy.16
  222.1 6.4 %convolution_multiply_fusion.1 = f32[624,104]{0,1:T(8,128)S(1)} fusion(bf16[6656,104]{1,0:T(8,128)(2,1)} %bitcast.98, f32[]{:T(128)} %bitcast.7, bf16[1,6656,624]{1,2,0:T(8,128)(2,1)} %param.3), kind=kOutput, calls=%fused_computation.7 | convolution fusion | flops 863960448 | bytes 9950724 | tf_op jit(solution)/shard_map/dot_general | solution.py:17
  228.6 23.2 %fusion.23 = f32[8,8,6]{1,0,2:T(8,128)S(1)} fusion(bf16[8,832,6,104]{1,0,3,2:T(8,128)(2,1)} %reshape_squeeze.14, bf16[8,832,104]{1,0,2:T(8,128)(2,1)S(1)} %copy-done.2, f32[]{:T(128)} %bitcast.7), kind=kOutput, calls=%fused_computation.16 | convolution fusion | flops 66454272 | bytes 9692676 | tf_op jit(solution)/shard_map/ipra,jpa->rij/dot_general | solution.py:22
  251.8 0.0 collective-permute-done.1
  251.8 5.9 %convolution_multiply_fusion = f32[624,104]{0,1:T(8,128)S(1)} fusion(bf16[6656,624]{0,1:T(8,128)(2,1)} %collective-permute-done.1, bf16[6656,104]{1,0:T(8,128)(2,1)S(1)} %bitcast.96, f32[]{:T(128)} %bitcast.9), kind=kOutput, calls=%fused_computation.6 | convolution fusion | flops 863960448 | bytes 9950724 | tf_op jit(solution)/shard_map/dot_general | solution.py:17
  257.7 0.0 collective-permute-done
  257.7 6.1 %fusion.7 = f32[624,104]{0,1:T(8,128)S(1)} fusion(f32[624,104]{0,1:T(8,128)S(1)} %convolution_multiply_fusion, f32[624,104]{0,1:T(8,128)S(1)} %convolution_multiply_fusion.1, bf16[6656,624]{0,1:T(8,128)(2,1)} %collective-permute-done, bf16[6656,104]{1,0:T(8,128)(2,1)S(1)} %bitcast.94, f32[]{:T(128)} %bitcast.4), kind=kOutput, calls=%fused_computation.10 | convolution fusion | flops 864090240 | bytes 10469892 | tf_op jit(solution)/shard_map/dot_general | solution.py:17
  263.8 0.2 copy.8
  263.9 1.2 add.60
  265.1 15.4 %reshape.118 = bf16[8,832,6,104]{1,0,3,2:T(8,128)(2,1)} reshape(bf16[6656,624]{0,1:T(8,128)(2,1)} %collective-permute-done.1) | data formatting | bytes 16613376 | tf_op jit(solution)/shard_map/reshape | solution.py:20
  280.5 23.2 %fusion.32 = f32[8,8,6]{1,0,2:T(8,128)S(1)} fusion(bf16[8,832,6,104]{1,0,3,2:T(8,128)(2,1)} %reshape.118, bf16[8,832,104]{1,0,2:T(8,128)(2,1)S(1)} %copy-done.1, f32[]{:T(128)} %bitcast.9), kind=kOutput, calls=%fused_computation.19 | convolution fusion | flops 66454272 | bytes 9692676 | tf_op jit(solution)/shard_map/ipra,jpa->rij/dot_general | solution.py:22
  303.7 15.4 %reshape.117 = bf16[8,832,6,104]{1,0,3,2:T(8,128)(2,1)} reshape(bf16[6656,624]{0,1:T(8,128)(2,1)} %collective-permute-done) | data formatting | bytes 16613376 | tf_op jit(solution)/shard_map/reshape | solution.py:20
  319.1 23.2 %fusion.41 = f32[6,8,8]{1,2,0:T(8,128)S(1)} fusion(f32[8,8,6]{1,0,2:T(8,128)S(1)} %fusion.32, f32[8,8,6]{1,0,2:T(8,128)S(1)} %fusion.23, bf16[8,832,6,104]{1,0,3,2:T(8,128)(2,1)} %reshape.117, bf16[8,832,104]{1,0,2:T(8,128)(2,1)S(1)} %copy-done, f32[]{:T(128)} %bitcast.4), kind=kOutput, calls=%fused_computation.22 | convolution fusion | flops 66455040 | bytes 9695748 | tf_op jit(solution)/shard_map/ipra,jpa->rij/dot_general | solution.py:22
  342.3 0.1 copy.12
  342.4 0.7 add.64
  (8 shorter events, 0.0 us)
Async XLA Ops:
  0.6 208.2 %all-to-all-start = ((bf16[16,3,416,104]{3,2,1,0:T(8,128)(2,1)}), bf16[16,3,416,104]{3,2,1,0:T(8,128)(2,1)}, u32[]{:S(2)}, u32[]{:S(2)}) async-start(bf16[16,3,416,104]{3,2,1,0:T(8,128)(2,1)} %param.4), calls=%async_computation | async-start | bytes 10223616 | tf_op jit(solution)/shard_map/all_to_all | solution.py:38
  7.2 244.6 %collective-permute-start.1 = (bf16[6656,624]{0,1:T(8,128)(2,1)}, bf16[6656,624]{0,1:T(8,128)(2,1)}, u32[]{:S(2)}, u32[]{:S(2)}) collective-permute-start(bf16[6656,624]{0,1:T(8,128)(2,1)} %bitcast.91), channel_id=1, source_target_pairs={{0,15},{1,0},{2,1},{3,2},{4,3},{5,4},{6,5},{7,6},{8,7},{9,8},{10,9... | collective-permute-start | bytes 24920072 | tf_op jit(solution)/shard_map/ppermute | solution.py:13
  7.6 250.1 %collective-permute-start = (bf16[6656,624]{0,1:T(8,128)(2,1)}, bf16[6656,624]{0,1:T(8,128)(2,1)}, u32[]{:S(2)}, u32[]{:S(2)}) collective-permute-start(bf16[6656,624]{0,1:T(8,128)(2,1)} %bitcast.92), channel_id=1, source_target_pairs={{0,1},{1,2},{2,3},{3,4},{4,5},{5,6},{6,7},{7,8},{8,9},{9,10},{10,1... | collective-permute-start | bytes 24920072 | tf_op jit(solution)/shard_map/ppermute | solution.py:13
  9.8 15.3 %copy-start.3 = (s32[16,3]{0,1:T(4,128)S(1)}, s32[16,3]{0,1:T(4,128)}, u32[]{:S(2)}) copy-start(s32[16,3]{0,1:T(4,128)} %param.5) | copy-start | bytes 580
  222.1 6.4 %copy-start.2 = (bf16[8,832,104]{1,0,2:T(8,128)(2,1)S(1)}, bf16[8,832,104]{1,0,2:T(8,128)(2,1)}, u32[]{:S(2)}) copy-start(bf16[8,832,104]{1,0,2:T(8,128)(2,1)} %copy.17) | copy-start | bytes 4153348
  265.1 15.4 %copy-start.1 = (bf16[8,832,104]{1,0,2:T(8,128)(2,1)S(1)}, bf16[8,832,104]{1,0,2:T(8,128)(2,1)}, u32[]{:S(2)}) copy-start(bf16[8,832,104]{1,0,2:T(8,128)(2,1)} %copy.18) | copy-start | bytes 4153348
  303.7 15.4 %copy-start = (bf16[8,832,104]{1,0,2:T(8,128)(2,1)S(1)}, bf16[8,832,104]{1,0,2:T(8,128)(2,1)}, u32[]{:S(2)}) copy-start(bf16[8,832,104]{1,0,2:T(8,128)(2,1)} %copy.16) | copy-start | bytes 4153348
where the time goes:
time: 345 us; the launch traced here: 343 us
  waiting for transfers between devices  181 us (52%)
  matrix products  87.9 us (25%)
  local copies, waits for them, and re-layouts  62.2 us (18%)
  starting transfers between devices  9.21 us (3%)
    all_to_all x1, waiting for transfers between devices, local(): lax.all_to_all(right_amps, 'ka', split_axis=0, concat_axis=2, tiled=True)[0]  181 us
    dot_general x3, matrix products, contract(): jnp.einsum('ipra,jpa->rij', left_view, right_view, preferred_element_type...  69.5 us
    reshape x2, local copies, waits for them, and re-layouts, contract(): left_view = left_block.reshape(NO, NO * NV, NL, NV)  30.8 us
    dot_general x3, matrix products, contract(): lax.dot_general(left_block, right_block, (((0,), (0,)), ((), ())), prefer...  18.4 us
    another operation x1, local copies, waits for them, and re-layouts, contract(): left_view = left_block.reshape(NO, NO * NV, NL, NV)  15.3 us
    another operation x3, local copies, waits for them, and re-layouts, contract(): right_view = right_block.reshape(NO, NO * NV, NV)  9.29 us
  transfers between devices with their start and end apart: 3, of which 1 were waited for; matrix products, arithmetic and copies ran while one was open for 19% of the time, Pallas kernels for 0%

commit v1 on v0

v1 whole, which is shorter than its diff:
```python
import jax
import jax.numpy as jnp
from jax import lax
from jax.sharding import PartitionSpec as P

NO = 8
NV = 104
NL = 6


def shifted(block, by):
    length = lax.axis_size("ka")
    return lax.ppermute(block, "ka", [(i, (i + by) % length) for i in range(length)])


def local(left_amps, right_amps, allowed):
    windows = right_amps.shape[1]
    middle = windows // 2
    count = lax.axis_size("ka")
    position = lax.axis_index("ka")
    lined = jnp.stack(
        [jnp.roll(right_amps[:, w], w - middle, axis=0) for w in range(windows)], axis=1
    )
    relaid = lax.all_to_all(lined, "ka", split_axis=0, concat_axis=2, tiled=True)[0]
    left = left_amps[0]
    right = relaid.transpose(1, 0, 2).reshape(-1, windows * NV)
    square = lax.dot_general(
        left, right, (((0,), (0,)), ((), ())), preferred_element_type=jnp.float32
    ).reshape(NL * NV, windows, NV)
    occupied = -jnp.einsum(
        "ipra,wjpa->wrij",
        left.reshape(NO, NO * NV, NL, NV),
        relaid.reshape(windows, NO, NO * NV, NV),
        preferred_element_type=jnp.float32,
    )
    total_vv = 0.0
    total_oo = 0.0
    for w in range(windows):
        point = (position - (w - middle)) % count
        factor = allowed[point, w].astype(jnp.float32)
        vv = (square[:, w] * factor).reshape(-1)
        oo = (occupied[w] * factor).reshape(-1)
        if w != middle:
            vv = shifted(vv, middle - w)
            oo = shifted(oo, middle - w)
        total_vv = total_vv + vv
        total_oo = total_oo + oo
    return (total_vv[None], total_oo[None])


def solution(mesh):
    in_specs = (P(("grp", "ka"), None, None), P("grp", None, "ka", None), P("grp", None))
    out_specs = (P(("grp", "ka"), None), P(("grp", "ka"), None))
    return jax.shard_map(local, mesh=mesh, in_specs=in_specs, out_specs=out_specs, check_vma=False)
```

time: 345 us -> 200 us (0.58)
  the two profiles are of different devices: /device:TPU:13 before, /device:TPU:0 now
where the time goes in v1:
time: 200 us; the launch traced here: 199 us
  waiting for transfers between devices  81 us (40%)
  local copies, waits for them, and re-layouts  49.7 us (25%)
  matrix products  30.8 us (15%)
  starting transfers between devices  30.3 us (15%)
  other arithmetic  4.33 us (2%)
  between operations  2.73 us (1%)
    all_to_all x1, waiting for transfers between devices, local(): lax.all_to_all(lined, 'ka', split_axis=0, concat_axis=2, tiled=True)[0]  75.8 us
    ppermute x4, starting transfers between devices, shifted(): lax.ppermute(block, 'ka', [(i, (i + by) % length) for i in range(length)])  22.8 us
    dot_general x1, matrix products, local(): jnp.einsum('ipra,wjpa->wrij', left.reshape(NO, NO * NV, NL, NV), relaid.r...  22.8 us
    another operation x1, local copies, waits for them, and re-layouts, local(): left.reshape(NO, NO * NV, NL, NV)  15.3 us
    squeeze x1, local copies, waits for them, and re-layouts, local(): lax.all_to_all(lined, 'ka', split_axis=0, concat_axis=2, tiled=True)[0]  9.52 us
    another operation x1, local copies, waits for them, and re-layouts, local(): relaid.reshape(windows, NO, NO * NV, NV)  8.79 us
    all_to_all x1, local copies, waits for them, and re-layouts, local(): lax.all_to_all(lined, 'ka', split_axis=0, concat_axis=2, tiled=True)[0]  8.48 us
    dot_general x1, matrix products, local(): lax.dot_general(left, right, (((0,), (0,)), ((), ())), preferred_element_...  8.01 us
  transfers between devices with their start and end apart: 5, of which 3 were waited for; matrix products, arithmetic and copies ran while one was open for 20% of the time, Pallas kernels for 0%

profile of v1, /device:TPU:0, one launch (start us, length us, event | category | flops | bytes accessed | tf_op | source)
XLA Modules:
  0.0 198.9 jit_solution(14873334496904998398)
XLA Ops:
  0.6 1.0 slice_bitcast_fusion.3
  1.6 2.1 %slice_bitcast_fusion.1 = (bf16[15,416,104]{2,1,0:T(8,128)(2,1)S(1)}, bf16[15,416,104]{2,1,0:T(8,128)(2,1)S(1)}) fusion(bf16[16,3,416,104]{3,2,1,0:T(8,128)(2,1)} %param.4), kind=kLoop, calls=%fused_computation.8 | loop fusion | bytes 5191680 | tf_op jit(solution)/shard_map/jit(_roll_static)/slice | solution.py:22
  3.7 0.8 maximum_bitcast_fusion
  4.5 0.7 slice-done
  5.2 3.4 %pad_maximum_fusion = bf16[16,3,416,104]{3,2,1,0:T(8,128)(2,1)} fusion(bf16[16,1,416,104]{3,2,1,0:T(8,128)(2,1)S(1)} %get-tuple-element.16, bf16[16,1,416,104]{3,2,1,0:T(8,128)(2,1)S(1)} %slice-done, bf16[16,1,416,104]{3,2,1,0:T(8,128)(2,1)S(1)} %get-tuple-element.15), kind=kLoop, calls=%fused_computation.2 | loop fusion | flops 4153344 | bytes 8306688 | tf_op jit(solution)/shard_map/stack | solution.py:21
  8.6 7.6 %all-to-all-start = ((bf16[16,3,416,104]{3,2,1,0:T(8,128)(2,1)}), bf16[16,3,416,104]{3,2,1,0:T(8,128)(2,1)}, u32[]{:S(2)}, u32[]{:S(2)}) async-start(bf16[16,3,416,104]{3,2,1,0:T(8,128)(2,1)} %pad_maximum_fusion), calls=%async_computation | async-start | bytes 10223616 | tf_op jit(solution)/shard_map/all_to_all | solution.py:24
  16.2 0.6 constant_dynamic-slice_fusion.2
  18.7 15.3 %reshape.46 = bf16[8,832,6,104,1]{1,0,3,2,4:T(8,128)(2,1)} reshape(bf16[1,6656,624]{1,2,0:T(8,128)(2,1)} %param.3) | data formatting | bytes 16613376 | tf_op jit(solution)/shard_map/reshape;squeeze | solution.py:32
  34.0 75.8 %all-to-all-done = bf16[16,3,416,104]{3,2,1,0:T(8,128)(2,1)} async-done(((bf16[16,3,416,104]{3,2,1,0:T(8,128)(2,1)}), bf16[16,3,416,104]{3,2,1,0:T(8,128)(2,1)}, u32[]{:S(2)}, u32[]{:S(2)}) %all-to-all-start) | async-done | bytes 4153376 | tf_op jit(solution)/shard_map/all_to_all | solution.py:24
  109.8 8.5 %copy.10 = bf16[1,3,16,416,104]{3,2,4,1,0:T(8,128)(2,1)} copy(bf16[1,3,16,416,104]{4,3,1,2,0:T(8,128)(2,1)} %bitcast.7) | data formatting | bytes 8306688 | tf_op jit(solution)/shard_map/all_to_all | solution.py:24
  118.3 9.5 %squeeze.4 = bf16[3,6656,104]{1,2,0:T(8,128)(2,1)} reshape(bf16[1,3,16,416,104]{3,2,4,1,0:T(8,128)(2,1)} %copy.10) | data formatting | bytes 8306688 | tf_op jit(solution)/shard_map/squeeze | solution.py:24
  127.8 8.8 %reshape.45 = bf16[3,8,832,104,1]{2,1,3,0,4:T(8,128)(2,1)} reshape(bf16[1,3,16,416,104]{3,2,4,1,0:T(8,128)(2,1)} %copy.10) | data formatting | bytes 8306688 | tf_op jit(solution)/shard_map/reshape;squeeze | solution.py:33
  136.6 8.0 %fusion = f32[312,624]{1,0:T(8,128)S(1)} fusion(bf16[6656,312]{0,1:T(8,128)(2,1)} %bitcast.73, bf16[1,6656,624]{1,2,0:T(8,128)(2,1)} %param.3), kind=kOutput, calls=%fused_computation | convolution fusion | flops 2591686656 | bytes 13238784 | tf_op jit(solution)/shard_map/dot_general | solution.py:27
  145.1 0.3 mul.62
  145.3 0.8 collective-permute-start
  146.4 0.3 mul.68
  146.6 21.3 %collective-permute-start.1 = (f32[64896]{0:T(1024)S(1)}, f32[64896]{0:T(1024)S(1)}, u32[]{:S(2)}, u32[]{:S(2)}) collective-permute-start(f32[64896]{0:T(1024)S(1)} %mul.68), channel_id=1, source_target_pairs={{0,15},{1,0},{2,1},{3,2},{4,3},{5,4},{6,5},{7,6},{8,7},{9,8},{10,9... | collective-permute-start | bytes 778760 | tf_op jit(solution)/shard_map/ppermute | solution.py:13
  168.0 22.8 %fusion.10 = f32[3,6,8,8]{2,3,1,0:T(8,128)S(1)} fusion(bf16[8,832,6,104,1]{1,0,3,2,4:T(8,128)(2,1)} %reshape.46, bf16[3,8,832,104,1]{2,1,3,0,4:T(8,128)(2,1)} %reshape.45), kind=kOutput, calls=%fused_computation.11 | convolution fusion | flops 199361664 | bytes 12464640 | tf_op jit(solution)/shard_map/ipra,wjpa->wrij/dot_general | solution.py:30
  190.9 0.5 collective-permute-start.3
  191.7 0.3 mul.65
  192.2 0.6 collective-permute-done.3
  192.8 4.6 %collective-permute-done.2 = f32[384]{0:T(512)S(1)} collective-permute-done((f32[384]{0:T(512)S(1)}, f32[384]{0:T(512)S(1)}, u32[]{:S(2)}, u32[]{:S(2)}) %collective-permute-start.2) | collective-permute-done | bytes 1568 | tf_op jit(solution)/shard_map/ppermute | solution.py:13
  197.4 0.6 broadcast_in_dim.7
  198.0 0.9 broadcast_in_dim.6
  (22 shorter events, 1.3 us)
Async XLA Ops:
  3.7 1.5 slice-start
  8.6 7.6 %copy-start = (s32[16,3]{0,1:T(4,128)S(1)}, s32[16,3]{0,1:T(4,128)}, u32[]{:S(2)}) copy-start(s32[16,3]{0,1:T(4,128)} %param.5) | copy-start | bytes 580
  8.6 101.2 %all-to-all-start = ((bf16[16,3,416,104]{3,2,1,0:T(8,128)(2,1)}), bf16[16,3,416,104]{3,2,1,0:T(8,128)(2,1)}, u32[]{:S(2)}, u32[]{:S(2)}) async-start(bf16[16,3,416,104]{3,2,1,0:T(8,128)(2,1)} %pad_maximum_fusion), calls=%async_computation | async-start | bytes 10223616 | tf_op jit(solution)/shard_map/all_to_all | solution.py:24
  145.3 52.6 %collective-permute-start = (f32[64896]{0:T(1024)S(1)}, f32[64896]{0:T(1024)S(1)}, u32[]{:S(2)}, u32[]{:S(2)}) collective-permute-start(f32[64896]{0:T(1024)S(1)} %mul.62), channel_id=1, source_target_pairs={{0,1},{1,2},{2,3},{3,4},{4,5},{5,6},{6,7},{7,8},{8,9},{9,10},{10,1... | collective-permute-start | bytes 778760 | tf_op jit(solution)/shard_map/ppermute | solution.py:13
  146.6 51.4 %collective-permute-start.1 = (f32[64896]{0:T(1024)S(1)}, f32[64896]{0:T(1024)S(1)}, u32[]{:S(2)}, u32[]{:S(2)}) collective-permute-start(f32[64896]{0:T(1024)S(1)} %mul.68), channel_id=1, source_target_pairs={{0,15},{1,0},{2,1},{3,2},{4,3},{5,4},{6,5},{7,6},{8,7},{9,8},{10,9... | collective-permute-start | bytes 778760 | tf_op jit(solution)/shard_map/ppermute | solution.py:13
  190.9 1.9 collective-permute-start.3
  191.6 5.8 %collective-permute-start.2 = (f32[384]{0:T(512)S(1)}, f32[384]{0:T(512)S(1)}, u32[]{:S(2)}, u32[]{:S(2)}) collective-permute-start(f32[384]{0:T(512)S(1)} %mul.71), channel_id=1, source_target_pairs={{0,1},{1,2},{2,3},{3,4},{4,5},{5,6},{6,7},{7,8},{8,9},{9,10},{10,1... | collective-permute-start | bytes 4616 | tf_op jit(solution)/shard_map/ppermute | solution.py:13

commit v2 on v1

--- a/solution.py
+++ b/solution.py
@@ -1,11 +1,256 @@
+import functools
+
 import jax
 import jax.numpy as jnp
 from jax import lax
+from jax.experimental import pallas as pl
+from jax.experimental.pallas import tpu as pltpu
 from jax.sharding import PartitionSpec as P
 
 NO = 8
 NV = 104
 NL = 6
+W = 3
+LANES = 128
+GROUP = 8
+SPARE = (LANES - NV) // GROUP
+PIECES = NV // GROUP
+BLOCKS = -(-PIECES // SPARE)
+MESH = pl.DeviceIdType.MESH
+LEFT_COLUMNS = NL * NV
+COLUMN_TILES = -(-LEFT_COLUMNS // LANES)
+F32 = jnp.float32
+
+
+def tail_rows(rows):
+    return rows // (BLOCKS + 1) // 16 * 16
+
+
+def lane_index(rows):
+    return lax.broadcasted_iota(jnp.int32, (rows, LANES), 1)
+
+
+def pack(source, packed, rows):
+    tail = tail_rows(rows)
+    head = rows - tail
+    lane = lane_index(tail)
+    rest = jnp.concatenate(
+        [source[head:rows, :].astype(F32), jnp.zeros((tail, LANES - NV), F32)], axis=1
+    )
+    for block in range(BLOCKS):
+        row = block * tail
+        out = jnp.concatenate(
+            [source[row:row + tail, :].astype(F32), jnp.zeros((tail, LANES - NV), F32)], axis=1
+        )
+        for group in range(SPARE):
+            piece = group * BLOCKS + block
+            if piece < PIECES:
+                place = NV + GROUP * group
+                moved = pltpu.roll(rest, (place - GROUP * piece) % LANES, 1)
+                out = jnp.where((lane >= place) & (lane < place + GROUP), moved, out)
+        packed[row:row + tail, :] = out.astype(jnp.bfloat16)
+    done = BLOCKS * tail
+    if done < head:
+        packed[done:head, :] = jnp.concatenate(
+            [source[done:head, :], jnp.zeros((head - done, LANES - NV), jnp.bfloat16)], axis=1
+        )
+
+
+def unpack(packed, plain, rows):
+    tail = tail_rows(rows)
+    head = rows - tail
+    lane = lane_index(tail)
+    plain[0:head, :] = packed[0:head, :]
+    rest = jnp.zeros((tail, LANES), F32)
+    for block in range(BLOCKS):
+        value = packed[block * tail:(block + 1) * tail, :].astype(F32)
+        for group in range(SPARE):
+            piece = group * BLOCKS + block
+            if piece < PIECES:
+                start = GROUP * piece
+                moved = pltpu.roll(value, (start - NV - GROUP * group) % LANES, 1)
+                rest = jnp.where((lane >= start) & (lane < start + GROUP), moved, rest)
+    plain[head:rows, :] = rest.astype(jnp.bfloat16)
+
+
+def kernel(count, rows, left_hbm, right_hbm, allowed, vv_out, oo_out, left, right, packed, landed,
+           plain, tiled, vv, oo, leave, arrive, local_sem, send_sem, recv_sem, give_sem, take_sem):
+    me = lax.axis_index("ka")
+    half_count = count // 2
+
+    def partner(n):
+        step = lax.rem(n, 2) * ((n + 1) // 2) + (1 - lax.rem(n, 2)) * (half_count + n // 2)
+        place, bit = 0, 1
+        while bit < count:
+            place = place + lax.rem(lax.rem(me // bit, 2) + lax.rem(step // bit, 2), 2) * bit
+            bit *= 2
+        return place
+
+    def send(w, target):
+        return pltpu.make_async_remote_copy(
+            src_ref=packed.at[w, target], dst_ref=landed.at[w, me],
+            send_sem=send_sem.at[w, target], recv_sem=recv_sem.at[w, me],
+            device_id={"ka": target}, device_id_type=MESH)
+
+    def receive(w, source):
+        return pltpu.make_async_remote_copy(
+            src_ref=packed.at[w, source], dst_ref=landed.at[w, source],
+            send_sem=send_sem.at[w, source], recv_sem=recv_sem.at[w, source],
+            device_id={"ka": source}, device_id_type=MESH)
+
+    order = (0, 2, 1)
+    fetch = {w: pltpu.make_async_copy(right_hbm.at[:, w], right.at[w], local_sem.at[w]) for w in order}
+    for w in order:
+        fetch[w].start()
+    fetch_left = pltpu.make_async_copy(left_hbm, left, local_sem.at[W])
+    fetch_left.start()
+
+    barrier = pltpu.get_barrier_semaphore()
+
+    @pl.loop(0, count - 1)
+    def _(n):
+        pl.semaphore_signal(barrier, inc=1, device_id={"ka": partner(n)}, device_id_type=MESH)
+
+    vv[...] = jnp.zeros_like(vv)
+    oo[...] = jnp.zeros_like(oo)
+
+    for place, w in enumerate(order):
+        fetch[w].wait()
+        if place == 0:
+            pl.semaphore_wait(barrier, count - 1)
+
+        @pl.loop(0, count - 1)
+        def _(n):
+            target = partner(n)
+            point = lax.rem(target + count - (w - 1), count)
+            pack(right.at[w, point], packed.at[w, target], rows)
+            send(w, target).start()
+
+    fetch_left.wait()
+
+    def multiply(windows, source):
+        here = left.at[pl.ds(pl.multiple_of(source * rows, 16), rows), :]
+        for w in windows:
+            vv[w] += lax.dot_general(here[...], plain[w], (((0,), (0,)), ((), ())),
+                                     preferred_element_type=F32)
+        for w in windows:
+            @pl.loop(0, rows // 16)
+            def _(chunk):
+                at = pl.ds(pl.multiple_of(chunk * 16, 16), 16)
+                value = plain[w, at, :].astype(F32)
+                lane = lane_index(16)
+                for tile in range(COLUMN_TILES):
+                    skip = tile * LANES % NV
+                    first = pltpu.roll(value, (-skip) % LANES, 1) if skip else value
+                    then = pltpu.roll(value, (NV - skip) % LANES, 1)
+                    tiled[w, at, tile * LANES:(tile + 1) * LANES] = jnp.where(
+                        lane < NV - skip, first, then)
+
+        share = NO * rows // (NO * NV)
+        per_index = NO * NV // rows
+        outer = source // per_index
+        start = lax.rem(source, per_index) * rows
+
+        @pl.loop(0, NO)
+        def _(i):
+            def step(chunk, sums):
+                at = pl.ds(pl.multiple_of(i * (NO * NV) + start + chunk * 16, 16), 16)
+                value = left[at, :].astype(F32)
+                near = pl.ds(pl.multiple_of(chunk * 16, 16), 16)
+                out = []
+                for w, total in zip(windows, sums):
+                    product = value * tiled[w, near, :LEFT_COLUMNS]
+                    out.append(total + product[:8] + product[8:])
+                return tuple(out)
+
+            sums = lax.fori_loop(0, rows // 16, step,
+                                 tuple(jnp.zeros((8, LEFT_COLUMNS), F32) for _ in windows), unroll=2)
+            for w, total in zip(windows, sums):
+                oo[w, i, pl.ds(outer, 1), :] += jnp.sum(total, axis=0, keepdims=True)
+
+    def phase(windows):
+        for w in windows:
+            plain[w] = jnp.concatenate(
+                [right[w, lax.rem(me + count - (w - 1), count)],
+                 jnp.zeros((rows, LANES - NV), jnp.bfloat16)], axis=1)
+        multiply(windows, me)
+
+        @pl.loop(0, count - 1)
+        def _(n):
+            source = partner(n)
+            for w in windows:
+                receive(w, source).wait_recv()
+                unpack(landed.at[w, source], plain.at[w], rows)
+            multiply(windows, source)
+
+    column = lax.broadcasted_iota(jnp.int32, (8, LEFT_COLUMNS), 1)
+    vector = lax.broadcasted_iota(jnp.int32, (8, LEFT_COLUMNS), 0)
+    pick = ((column >= vector * NV) & (column < (vector + 1) * NV)).astype(F32)
+
+    def occupied(w):
+        return -lax.dot_general(pick, oo[w].reshape(NO * NO, LEFT_COLUMNS), (((1,), (1,)), ((), ())),
+                                precision=lax.Precision.HIGHEST, preferred_element_type=F32)
+
+    phase((0, 2))
+    moves = []
+    for slot, (w, target) in enumerate(((0, lax.rem(me + 1, count)), (2, lax.rem(me + count - 1, count)))):
+        leave[slot, 0:LEFT_COLUMNS, :] = vv[w]
+        leave[slot, LEFT_COLUMNS:LEFT_COLUMNS + 8, 0:NO * NO] = occupied(w)
+        leave[slot, LEFT_COLUMNS:LEFT_COLUMNS + 8, NO * NO:] = jnp.zeros((8, LANES - NO * NO), F32)
+        move = pltpu.make_async_remote_copy(
+            src_ref=leave.at[slot], dst_ref=arrive.at[slot], send_sem=give_sem.at[slot],
+            recv_sem=take_sem.at[slot], device_id={"ka": target}, device_id_type=MESH)
+        move.start()
+        moves.append(move)
+    phase((1,))
+    for move in moves:
+        move.wait()
+    factor = [allowed[me, w].astype(F32) for w in range(W)]
+    vv_out[...] = (factor[1] * vv[1] + factor[0] * arrive[0, 0:LEFT_COLUMNS, :]
+                   + factor[2] * arrive[1, 0:LEFT_COLUMNS, :])[:, :NV]
+    oo_out[...] = (factor[1] * occupied(1)
+                   + factor[0] * arrive[0, LEFT_COLUMNS:LEFT_COLUMNS + 8, 0:NO * NO]
+                   + factor[2] * arrive[1, LEFT_COLUMNS:LEFT_COLUMNS + 8, 0:NO * NO])
+    for w in order:
+        @pl.loop(0, count - 1)
+        def _(n):
+            send(w, partner(n)).wait_send()
+
+
+def kernel_local(left_amps, right_amps, allowed):
+    count, _, rows, _ = right_amps.shape
+    all_rows = left_amps.shape[1]
+    vv, oo = pl.pallas_call(
+        functools.partial(kernel, count, rows),
+        out_shape=(jax.ShapeDtypeStruct((LEFT_COLUMNS, NV), F32),
+                   jax.ShapeDtypeStruct((8, NO * NO), F32)),
+        in_specs=[pl.BlockSpec(memory_space=pl.ANY), pl.BlockSpec(memory_space=pl.ANY),
+                  pl.BlockSpec(memory_space=pltpu.SMEM)],
+        out_specs=[pl.BlockSpec(memory_space=pltpu.VMEM)] * 2,
+        scratch_shapes=[
+            pltpu.VMEM((all_rows, LEFT_COLUMNS), jnp.bfloat16),
+            pltpu.VMEM((W, count, rows, NV), jnp.bfloat16),
+            pltpu.VMEM((W, count, rows - tail_rows(rows), LANES), jnp.bfloat16),
+            pltpu.VMEM((W, count, rows - tail_rows(rows), LANES), jnp.bfloat16),
+            pltpu.VMEM((W, rows, LANES), jnp.bfloat16),
+            pltpu.VMEM((W, rows, COLUMN_TILES * LANES), F32),
+            pltpu.VMEM((W, LEFT_COLUMNS, LANES), F32),
+            pltpu.VMEM((W, NO, NO, LEFT_COLUMNS), F32),
+            pltpu.VMEM((2, LEFT_COLUMNS + 8, LANES), F32),
+            pltpu.VMEM((2, LEFT_COLUMNS + 8, LANES), F32),
+            pltpu.SemaphoreType.DMA((W + 1,)),
+            pltpu.SemaphoreType.DMA((W, count)),
+            pltpu.SemaphoreType.DMA((W, count)),
+            pltpu.SemaphoreType.DMA((2,)),
+            pltpu.SemaphoreType.DMA((2,)),
+        ],
+        compiler_params=pltpu.CompilerParams(
+            collective_id=0, has_side_effects=True, vmem_limit_bytes=56 * 1024 * 1024),
+        cost_estimate=pl.CostEstimate(
+            flops=2 * W * all_rows * LEFT_COLUMNS * NV, transcendentals=0,
+            bytes_accessed=2 * all_rows * (LEFT_COLUMNS + W * NV)),
+    )(left_amps[0], right_amps, allowed)
+    return (vv.reshape(1, -1), oo[:NL].reshape(1, -1))
 
 
 def shifted(block, by):
@@ -13,7 +258,7 @@
     return lax.ppermute(block, "ka", [(i, (i + by) % length) for i in range(length)])
 
 
-def local(left_amps, right_amps, allowed):
+def plain_local(left_amps, right_amps, allowed):
     windows = right_amps.shape[1]
     middle = windows // 2
     count = lax.axis_size("ka")
@@ -48,6 +293,13 @@
     return (total_vv[None], total_oo[None])
 
 
+def local(left_amps, right_amps, allowed):
+    count, _, rows, _ = right_amps.shape
+    if rows % 16 == 0 and (NO * NV) % rows == 0 and count & (count - 1) == 0:
+        return kernel_local(left_amps, right_amps, allowed)
+    return plain_local(left_amps, right_amps, allowed)
+
+
 def solution(mesh):
     in_specs = (P(("grp", "ka"), None, None), P("grp", None, "ka", None), P("grp", None))
     out_specs = (P(("grp", "ka"), None), P(("grp", "ka"), None))

time: 200 us -> 263 us (1.31)
  Pallas kernels: 0 us -> 245 us
  waiting for transfers between devices: 81 us -> 0 us
  local copies, waits for them, and re-layouts: 49.7 us -> 16.9 us
  matrix products: 30.8 us -> 0 us
  starting transfers between devices: 30.3 us -> 0 us
  other arithmetic: 4.33 us -> 0 us
    pallas_call x0 -> x1, Pallas kernels: none -> 245 us  [kernel_local(): pl.pallas_call(functools.partial(kernel, count, rows), out_shape=(jax.Sha...]
    all_to_all x1 -> x0, waiting for transfers between devices: 75.8 us -> none  [local(): lax.all_to_all(lined, 'ka', split_axis=0, concat_axis=2, tiled=True)[0]]
    dot_general x2 -> x0, matrix products: 30.8 us -> none  [the longest x1 22.8 us: local(): jnp.einsum('ipra,wjpa->wrij', left.reshape(NO, NO * NV, NL, NV), relaid.r...]
    another operation x2 -> x0, local copies, waits for them, and re-layouts: 24.1 us -> none  [the longest x1 15.3 us: local(): left.reshape(NO, NO * NV, NL, NV)]
    ppermute x4 -> x0, starting transfers between devices: 22.8 us -> none  [shifted(): lax.ppermute(block, 'ka', [(i, (i + by) % length) for i in range(length)])]
    unnamed x5 -> x2, local copies, waits for them, and re-layouts: 0.49 us -> 13.4 us
    squeeze x1 -> x0, local copies, waits for them, and re-layouts: 9.52 us -> none  [local(): lax.all_to_all(lined, 'ka', split_axis=0, concat_axis=2, tiled=True)[0]]
    all_to_all x1 -> x0, local copies, waits for them, and re-layouts: 8.48 us -> none  [local(): lax.all_to_all(lined, 'ka', split_axis=0, concat_axis=2, tiled=True)[0]]
  transfers between devices with their start and end apart: 5 -> 0, of which waited for: 3 -> 0; matrix products, arithmetic and copies ran while one was open for 20% -> 0% of each run, Pallas kernels for 0% -> 0%
where the time goes in v2:
time: 263 us; the launch traced here: 262 us
  Pallas kernels  245 us (93%)
  local copies, waits for them, and re-layouts  16.9 us (6%)
    pallas_call x1, Pallas kernels, kernel_local(): pl.pallas_call(functools.partial(kernel, count, rows), out_shape=(jax.Sha...  245 us
    unnamed x2, local copies, waits for them, and re-layouts  13.4 us

profile of v2, /device:TPU:0, one launch (start us, length us, event | category | flops | bytes accessed | tf_op | source)
XLA Modules:
  0.0 262.3 jit_solution(15285573807360665580)
XLA Ops:
  0.6 1.4 copy.8.allowed
  2.0 12.1 %copy.7 = bf16[1,6656,624]{2,1,0:T(8,128)(2,1)} copy(bf16[1,6656,624]{1,2,0:T(8,128)(2,1)} %param.3) | data formatting | bytes 16613376 | tf_op args[0]
  14.1 244.8 %shard_map.50 = (f32[624,104]{1,0:T(8,128)}, f32[8,64]{1,0:T(8,128)}) custom-call(bf16[6656,624]{1,0:T(8,128)(2,1)} %bitcast.2, bf16[16,3,416,104]{3,2,1,0:T(8,128)(2,1)} %right_hbm.1, s32[16,3]{1,0:T(8,128)} %copy.8.allowed), custom_call_target="tpu_custom_call" | custom-call | flops 2591686656 | bytes 12460032 | tf_op jit(solution)/shard_map/pallas_call | solution.py:223
  258.9 2.1 reshape.10
  261.0 1.3 reshape.11

commit v3 on v1

--- a/solution.py
+++ b/solution.py
@@ -1,11 +1,249 @@
+import functools
+
 import jax
 import jax.numpy as jnp
 from jax import lax
+from jax.experimental import pallas as pl
+from jax.experimental.pallas import tpu as pltpu
 from jax.sharding import PartitionSpec as P
 
 NO = 8
 NV = 104
 NL = 6
+W = 3
+LANES = 128
+GROUP = 8
+SPARE = (LANES - NV) // GROUP
+PIECES = NV // GROUP
+BLOCKS = -(-PIECES // SPARE)
+MESH = pl.DeviceIdType.MESH
+LEFT_COLUMNS = NL * NV
+PAIR = 2
+F32 = jnp.float32
+
+
+def tail_rows(rows):
+    return rows // (BLOCKS + 1) // 16 * 16
+
+
+def lane_index(rows):
+    return lax.broadcasted_iota(jnp.int32, (rows, LANES), 1)
+
+
+def pack(source, packed, rows):
+    tail = tail_rows(rows)
+    head = rows - tail
+    lane = lane_index(tail)
+    rest = jnp.concatenate(
+        [source[head:rows, :].astype(F32), jnp.zeros((tail, LANES - NV), F32)], axis=1
+    )
+    for block in range(BLOCKS):
+        row = block * tail
+        out = jnp.concatenate(
+            [source[row:row + tail, :].astype(F32), jnp.zeros((tail, LANES - NV), F32)], axis=1
+        )
+        for group in range(SPARE):
+            piece = group * BLOCKS + block
+            if piece < PIECES:
+                place = NV + GROUP * group
+                moved = pltpu.roll(rest, (place - GROUP * piece) % LANES, 1)
+                out = jnp.where((lane >= place) & (lane < place + GROUP), moved, out)
+        packed[row:row + tail, :] = out.astype(jnp.bfloat16)
+    done = BLOCKS * tail
+    if done < head:
+        packed[done:head, :] = jnp.concatenate(
+            [source[done:head, :], jnp.zeros((head - done, LANES - NV), jnp.bfloat16)], axis=1
+        )
+
+
+def unpack(packed, plain, first, lanes, rows):
+    tail = tail_rows(rows)
+    head = rows - tail
+    lane = lane_index(tail)
+    plain[pl.ds(first, head), lanes] = packed[0:head, :]
+    rest = jnp.zeros((tail, LANES), F32)
+    for block in range(BLOCKS):
+        value = packed[block * tail:(block + 1) * tail, :].astype(F32)
+        for group in range(SPARE):
+            piece = group * BLOCKS + block
+            if piece < PIECES:
+                start = GROUP * piece
+                moved = pltpu.roll(value, (start - NV - GROUP * group) % LANES, 1)
+                rest = jnp.where((lane >= start) & (lane < start + GROUP), moved, rest)
+    plain[pl.ds(pl.multiple_of(first + head, 16), tail), lanes] = rest.astype(jnp.bfloat16)
+
+
+def kernel(count, rows, left_hbm, right_hbm, allowed, vv_out, oo_out, left, right, packed, landed,
+           plain, vv, oo, leave, arrive, local_sem, send_sem, recv_sem, give_sem, take_sem):
+    me = lax.axis_index("ka")
+    chips = count // PAIR
+    half = chips // 2
+    sibling = me + 1 - 2 * lax.rem(me, PAIR)
+    span = NO * NV
+    edge = (-span) % LANES
+
+    def other_chip(n):
+        step = lax.rem(n, 2) * ((n + 1) // 2) + (1 - lax.rem(n, 2)) * (half + n // 2)
+        chip, place, bit = me // PAIR, 0, 1
+        while bit < chips:
+            place = place + lax.rem(lax.rem(chip // bit, 2) + lax.rem(step // bit, 2), 2) * bit
+            bit *= 2
+        return place
+
+    def send(target):
+        return pltpu.make_async_remote_copy(
+            src_ref=packed.at[target], dst_ref=landed.at[me],
+            send_sem=send_sem.at[target], recv_sem=recv_sem.at[me],
+            device_id={"ka": target}, device_id_type=MESH)
+
+    def receive(source):
+        return pltpu.make_async_remote_copy(
+            src_ref=packed.at[source], dst_ref=landed.at[source],
+            send_sem=send_sem.at[source], recv_sem=recv_sem.at[source],
+            device_id={"ka": source}, device_id_type=MESH)
+
+    fetch = pltpu.make_async_copy(right_hbm, right, local_sem.at[0])
+    fetch.start()
+    fetch_left = pltpu.make_async_copy(left_hbm, left, local_sem.at[1])
+    fetch_left.start()
+
+    barrier = pltpu.get_barrier_semaphore()
+
+    @pl.loop(1, count)
+    def _(n):
+        pl.semaphore_signal(barrier, inc=1, device_id={"ka": lax.rem(me + n, count)},
+                            device_id_type=MESH)
+
+    plain[...] = jnp.zeros_like(plain)
+    vv[...] = jnp.zeros_like(vv)
+    oo[...] = jnp.zeros_like(oo)
+    fetch.wait()
+
+    def prepare(target):
+        for w in range(W):
+            point = lax.rem(target + count - (w - W // 2), count)
+            pack(right.at[point, w], packed.at[target, w], rows)
+
+    for n in range(chips - 1):
+        for core in range(PAIR):
+            target = other_chip(n) * PAIR + core
+            prepare(target)
+            if n == 0 and core == 0:
+                pl.semaphore_wait(barrier, count - 1)
+            send(target).start()
+        if n == 0:
+            prepare(sibling)
+            send(sibling).start()
+    fetch_left.wait()
+
+    row = lax.broadcasted_iota(jnp.int32, (LEFT_COLUMNS, LANES), 0)
+    column = lax.broadcasted_iota(jnp.int32, (LEFT_COLUMNS, LANES), 1)
+    same = lax.rem(row, NV) == column
+
+    def product(i, outer):
+        odd = lax.rem(i, 2)
+        at = pl.ds(pl.multiple_of(i * span - odd * edge, LANES), span + edge)
+        near = pl.ds(pl.multiple_of((1 - odd) * edge, 16), span + edge)
+        square = jnp.dot(left[:, at], plain[near, :], preferred_element_type=F32)
+        for w in range(W):
+            kept = jnp.where(same, square[:, w * LANES:(w + 1) * LANES], 0.0)
+            for r in range(NL):
+                oo[w, outer * NO + i, r:r + 1, :] = jnp.sum(
+                    kept[r * NV:(r + 1) * NV], axis=0, keepdims=True)
+        return square
+
+    def multiply(outer):
+        vv[...] += product(outer, outer)
+
+        @pl.loop(1, NO)
+        def _(n):
+            product(lax.rem(outer + n, NO), outer)
+
+    for w in range(W):
+        point = lax.rem(me + count - (w - W // 2), count)
+        plain[pl.ds(pl.multiple_of(edge + lax.rem(me, PAIR) * rows, 16), rows),
+              w * LANES:w * LANES + NV] = right[point, w]
+    receive(sibling).wait_recv()
+    for w in range(W):
+        unpack(landed.at[sibling, w], plain, pl.multiple_of(edge + lax.rem(sibling, PAIR) * rows, 16),
+               slice(w * LANES, (w + 1) * LANES), rows)
+    multiply(me // PAIR)
+
+    @pl.loop(0, chips - 1)
+    def _(n):
+        chip = other_chip(n)
+        for core in range(PAIR):
+            source = chip * PAIR + core
+            receive(source).wait_recv()
+            for w in range(W):
+                unpack(landed.at[source, w], plain, edge + core * rows,
+                       slice(w * LANES, (w + 1) * LANES), rows)
+        multiply(chip)
+
+    def occupied(w):
+        return -jnp.sum(oo[w], axis=2)
+
+    moves = []
+    for slot, (w, target) in enumerate(((0, lax.rem(me + 1, count)), (2, lax.rem(me + count - 1, count)))):
+        leave[slot, 0:LEFT_COLUMNS, :] = vv[:, w * LANES:(w + 1) * LANES]
+        leave[slot, LEFT_COLUMNS:, :] = jnp.concatenate(
+            [occupied(w), jnp.zeros((NO * NO, LANES - 8), F32)], axis=1)
+        move = pltpu.make_async_remote_copy(
+            src_ref=leave.at[slot], dst_ref=arrive.at[slot], send_sem=give_sem.at[slot],
+            recv_sem=take_sem.at[slot], device_id={"ka": target}, device_id_type=MESH)
+        move.start()
+        moves.append(move)
+    factor = [allowed[w, me].astype(F32) for w in range(W)]
+    centre = factor[1] * occupied(1)
+
+    @pl.loop(1, count)
+    def _(n):
+        send(lax.rem(me + n, count)).wait_send()
+
+    for move in moves:
+        move.wait()
+    vv_out[...] = (factor[1] * vv[:, LANES:2 * LANES] + factor[0] * arrive[0, 0:LEFT_COLUMNS, :]
+                   + factor[2] * arrive[1, 0:LEFT_COLUMNS, :])[:, :NV]
+    oo_out[...] = (centre + factor[0] * arrive[0, LEFT_COLUMNS:, 0:8]
+                   + factor[2] * arrive[1, LEFT_COLUMNS:, 0:8])
+
+
+def kernel_local(left_amps, right_amps, allowed):
+    count, _, rows, _ = right_amps.shape
+    all_rows = left_amps.shape[1]
+    head = rows - tail_rows(rows)
+    extent = NO * NV + 2 * ((-NO * NV) % LANES)
+    vv, oo = pl.pallas_call(
+        functools.partial(kernel, count, rows),
+        out_shape=(jax.ShapeDtypeStruct((LEFT_COLUMNS, NV), F32),
+                   jax.ShapeDtypeStruct((NO * NO, 8), F32)),
+        in_specs=[pl.BlockSpec(memory_space=pl.ANY), pl.BlockSpec(memory_space=pl.ANY),
+                  pl.BlockSpec(memory_space=pltpu.SMEM)],
+        out_specs=[pl.BlockSpec(memory_space=pltpu.VMEM)] * 2,
+        scratch_shapes=[
+            pltpu.VMEM((LEFT_COLUMNS, all_rows), jnp.bfloat16),
+            pltpu.VMEM((count, W, rows, NV), jnp.bfloat16),
+            pltpu.VMEM((count, W, head, LANES), jnp.bfloat16),
+            pltpu.VMEM((count, W, head, LANES), jnp.bfloat16),
+            pltpu.VMEM((extent, W * LANES), jnp.bfloat16),
+            pltpu.VMEM((LEFT_COLUMNS, W * LANES), F32),
+            pltpu.VMEM((W, NO * NO, 8, LANES), F32),
+            pltpu.VMEM((2, LEFT_COLUMNS + NO * NO, LANES), F32),
+            pltpu.VMEM((2, LEFT_COLUMNS + NO * NO, LANES), F32),
+            pltpu.SemaphoreType.DMA((2,)),
+            pltpu.SemaphoreType.DMA((count,)),
+            pltpu.SemaphoreType.DMA((count,)),
+            pltpu.SemaphoreType.DMA((2,)),
+            pltpu.SemaphoreType.DMA((2,)),
+        ],
+        compiler_params=pltpu.CompilerParams(
+            collective_id=0, has_side_effects=True, vmem_limit_bytes=56 * 1024 * 1024),
+        cost_estimate=pl.CostEstimate(
+            flops=2 * W * all_rows * LEFT_COLUMNS * NV * NO, transcendentals=0,
+            bytes_accessed=2 * all_rows * (LEFT_COLUMNS + W * NV)),
+    )(left_amps[0].T, right_amps, allowed.T)
+    oo = oo[:, :NL].reshape(NO, NO, NL).transpose(2, 1, 0)
+    return (vv.reshape(1, -1), oo.reshape(1, -1))
 
 
 def shifted(block, by):
@@ -13,7 +251,7 @@
     return lax.ppermute(block, "ka", [(i, (i + by) % length) for i in range(length)])
 
 
-def local(left_amps, right_amps, allowed):
+def plain_local(left_amps, right_amps, allowed):
     windows = right_amps.shape[1]
     middle = windows // 2
     count = lax.axis_size("ka")
@@ -48,6 +286,13 @@
     return (total_vv[None], total_oo[None])
 
 
+def local(left_amps, right_amps, allowed):
+    count, _, rows, _ = right_amps.shape
+    if rows % 16 == 0 and NO * NV == PAIR * rows and count == PAIR * NO:
+        return kernel_local(left_amps, right_amps, allowed)
+    return plain_local(left_amps, right_amps, allowed)
+
+
 def solution(mesh):
     in_specs = (P(("grp", "ka"), None, None), P("grp", None, "ka", None), P("grp", None))
     out_specs = (P(("grp", "ka"), None), P(("grp", "ka"), None))

time: 200 us -> 121 us (0.60)
  the two profiles are of different devices: /device:TPU:0 before, /device:TPU:24 now
where the time goes in v3:
time: 121 us
  Pallas kernels  116 us (96%)
  local copies, waits for them, and re-layouts  3.67 us (3%)
    pallas_call x1, Pallas kernels, kernel_local(): pl.pallas_call(functools.partial(kernel, count, rows), out_shape=(jax.Sha...  116 us
    reshape x2, local copies, waits for them, and re-layouts, kernel_local(): return (vv.reshape(1, -1), oo.reshape(1, -1))  2.78 us

profile of v3, /device:TPU:24, one launch (start us, length us, event | category | flops | bytes accessed | tf_op | source)
XLA Modules:
  0.0 120.7 jit_solution(8895520159919485024)
XLA Ops:
  0.6 116.4 %shard_map.50 = (f32[624,104]{1,0:T(8,128)}, f32[64,8]{1,0:T(8,128)}) custom-call(bf16[624,6656]{1,0:T(8,128)(2,1)} %bitcast.8, bf16[16,3,416,104]{3,2,1,0:T(8,128)(2,1)} %right_hbm.1, s32[3,16]{1,0:T(4,128)} %bitcast.9), custom_call_target="tpu_custom_call" | custom-call | flops 20733493248 | bytes 12460032 | tf_op jit(solution)/shard_map/pallas_call | solution.py:216
  117.0 2.1 %reshape.13 = f32[1,64896]{1,0:T(1,128)} reshape(f32[624,104]{1,0:T(8,128)} %get-tuple-element.4) | data formatting | bytes 519168 | tf_op jit(solution)/shard_map/reshape | solution.py:246
  119.1 0.8 slice_bitcast_fusion
  119.9 0.1 copy.6
  120.0 0.7 reshape.15
